TPU v7x, 128 devices: a whole 4x4x4 slice. The times are simulated.
128 devices in a mesh: fsdp: 16 (over y, x), exp: 8 (over z, core).
Axes of the slice: x: 4, y: 4, z: 4, core: 2. Of those that a mesh axis runs over, the one named last changes fastest.
Arguments:
- tokens: bfloat16 [16384, 3584], P(('fsdp', 'exp')), may hold values from -6 to 6
- grad_out: bfloat16 [16384, 3584], P(('fsdp', 'exp')), may hold values from -6 to 6
- route_probs: bfloat16 [16384, 2], P(('fsdp', 'exp')), may hold values from 0.19921875 to 1
- expert_ids: int32 [16384, 2], P(('fsdp', 'exp')), may hold values from 0 to 7, all different within a row; in each aligned block of 128 rows (0 to 127, 128 to 255, ...) at most 34 rows name the same one
- saved_pre: bfloat16 [8, 4352, 2, 2432], P('exp', None, None, 'fsdp'), may hold values from -6 to 6
- expert_weights: bfloat16 [8, 3584, 3, 2432], P('exp', None, None, 'fsdp'), may hold values from -0.09375 to 0.09375
Outputs:
- grad_tokens: bfloat16 [16384, 3584], P(('fsdp', 'exp'))
- expert_grad: bfloat16 [8, 3584, 3, 2432], P('exp', None, None, 'fsdp')
Inputs may be any that keep to these rules, and one draw needn't show every extreme that they name: `expert_ids`: A token's two experts differ. Among the 128 tokens of one device no expert is named more than 34 times, and in every draw some device names some expert exactly 34 times.
All inputs are finite; a program needn't handle non-finite values.
Results may differ from a plain program's by a relative error of at most 0.02.
Values may be sent and summed in bfloat16 or wider, within the bound.
A program may use at most 320 MiB of HBM per device.

v0:
```python
import jax
import jax.numpy as jnp
from jax import lax
from jax.sharding import PartitionSpec as P


def swiglu_back(gate_pre, up_pre, back):
    sig = jax.nn.sigmoid(gate_pre)
    act = gate_pre * sig
    hidden = act * up_pre
    d_gate = back * up_pre * sig * (1.0 + gate_pre * (1.0 - sig))
    d_up = back * act
    return (jnp.concatenate([d_gate, d_up], 1).astype(jnp.bfloat16), hidden)


def contract_rows(left, right):
    return lax.dot_general(
        left, right, (((0,), (0,)), ((), ())), preferred_element_type=jnp.float32
    )


def on_device(tokens, grad_out, route_probs, expert_ids, saved_pre, expert_weights):
    rows = tokens.shape[0]
    width = tokens.shape[1]
    experts = lax.axis_size("exp")
    capacity = 17 * rows // (8 * experts)
    flat_ids = expert_ids.reshape(-1)
    onehot = (flat_ids[:, None] == jnp.arange(experts, dtype=jnp.int32)[None, :]).astype(jnp.int32)
    before = jnp.cumsum(onehot, axis=0) - onehot
    slot = jnp.sum(before * onehot, axis=1)
    dest = (flat_ids * capacity + slot).reshape(rows, 2)
    x_buf = jnp.zeros((experts * capacity, width), jnp.bfloat16)
    x_buf = x_buf.at[dest[:, 0]].set(tokens).at[dest[:, 1]].set(tokens)
    dy_buf = jnp.zeros((experts * capacity, width), jnp.bfloat16)
    dy_buf = dy_buf.at[dest[:, 0]].set(grad_out).at[dest[:, 1]].set(grad_out)
    p_buf = jnp.zeros((experts * capacity,), jnp.bfloat16)
    p_buf = p_buf.at[dest[:, 0]].set(route_probs[:, 0]).at[dest[:, 1]].set(route_probs[:, 1])
    got_x, got_dy, got_p = (
        lax.all_to_all(
            x_buf.reshape(experts, capacity, width), "exp", split_axis=0, concat_axis=0, tiled=True
        ),
        lax.all_to_all(
            dy_buf.reshape(experts, capacity, width), "exp", split_axis=0, concat_axis=0, tiled=True
        ),
        lax.all_to_all(
            p_buf.reshape(experts, capacity), "exp", split_axis=0, concat_axis=0, tiled=True
        ),
    )
    all_x, all_dy, all_p = (
        lax.all_gather(got_x, "fsdp", axis=0, tiled=True),
        lax.all_gather(got_dy, "fsdp", axis=0, tiled=True),
        lax.all_gather(got_p, "fsdp", axis=0, tiled=True),
    )
    weights = expert_weights[0]
    share = weights.shape[2]
    pre = saved_pre[0]
    dys = all_dy.reshape(-1, width)
    ps = all_p.reshape(-1).astype(jnp.float32)
    back = ps[:, None] * jnp.dot(dys, weights[:, 2, :], preferred_element_type=jnp.float32)
    grads_in, hidden = swiglu_back(
        pre[:, 0, :].astype(jnp.float32), pre[:, 1, :].astype(jnp.float32), back
    )
    scaled = (ps[:, None] * hidden).astype(jnp.bfloat16)
    proj = weights[:, :2, :].reshape(width, 2 * share)
    summed = lax.psum_scatter(
        lax.dot_general(
            grads_in, proj, (((1,), (1,)), ((), ())), preferred_element_type=jnp.float32
        ).astype(jnp.bfloat16),
        "fsdp",
        scatter_dimension=0,
        tiled=True,
    )
    slot_dx = summed.reshape(experts, capacity, width)
    returned = lax.all_to_all(slot_dx, "exp", split_axis=0, concat_axis=0, tiled=True).reshape(
        -1, width
    )
    moe_dx = returned[dest[:, 0]].astype(jnp.float32) + returned[dest[:, 1]].astype(jnp.float32)
    xs = all_x.reshape(-1, width)
    first = contract_rows(xs, grads_in).reshape(width, 2, share)
    last = contract_rows(dys, scaled)
    grad = jnp.concatenate([first, last[:, None, :]], 1).astype(jnp.bfloat16)
    return (moe_dx.astype(jnp.bfloat16), grad[None])


def solution(mesh):
    in_specs = (
        P(("fsdp", "exp"), None),
        P(("fsdp", "exp"), None),
        P(("fsdp", "exp"), None),
        P(("fsdp", "exp"), None),
        P("exp", None, None, "fsdp"),
        P("exp", None, None, "fsdp"),
    )
    out_specs = (P(("fsdp", "exp"), None), P("exp", None, None, "fsdp"))
    return jax.shard_map(
        on_device, mesh=mesh, in_specs=in_specs, out_specs=out_specs, check_vma=False
    )
```

profile of v0, /device:TPU:1, one launch (start us, length us, event | category | flops | bytes accessed | tf_op | source)
XLA Modules:
  0.0 665.8 jit_solution(14745190977215942363)
XLA Ops:
  7.2 0.9 copy.35
  8.1 0.1 eq.29
  8.2 0.1 eq.25
  8.4 0.6 reduce-window.6
  9.0 0.2 slice_reduce_fusion
  9.2 0.1 fusion.30
  9.3 0.1 reduce_sum.12
  9.5 0.1 copy.37
  9.5 0.7 multiply_add_fusion
  10.2 3.1 scatter_custom_fusion.2
  13.4 2.9 scatter_fusion.1
  16.3 1.7 reshape.103
  17.9 35.5 %all_to_all.28 = bf16[8,34,3584]{2,1,0:T(8,128)(2,1)S(1)} all-to-all(bf16[8,34,3584]{2,1,0:T(8,128)(2,1)} %reshape.103), channel_id=1, replica_groups=mesh['fsdp'=16,'exp'=8] {'exp'}, dimensions={0} | all-to-all | bytes 3899392 | tf_op jit(solution)/shard_map/all_to_all | solution.py:42
  53.5 1.9 copy.40
  55.4 2.5 scatter_custom_fusion.4
  57.9 2.9 scatter_fusion.2
  60.8 1.7 reshape.108
  62.5 33.7 %all_to_all.29 = bf16[8,34,3584]{2,1,0:T(8,128)(2,1)S(1)} all-to-all(bf16[8,34,3584]{2,1,0:T(8,128)(2,1)} %reshape.108), channel_id=1, replica_groups=mesh['fsdp'=16,'exp'=8] {'exp'}, dimensions={0} | all-to-all | bytes 3899392 | tf_op jit(solution)/shard_map/all_to_all | solution.py:39
  96.2 1.8 copy.42
  98.1 1.3 scatter_custom_fusion
  99.4 1.3 scatter_fusion
  100.8 0.7 all_to_all.23
  101.5 4.1 all-to-all-start
  105.6 1.8 slice.54
  107.3 2.8 all-to-all-done
  110.1 20.5 %all-gather = bf16[128,1,34]{2,0,1:T(8,128)(2,1)S(1)} all-gather(bf16[8,1,34]{2,0,1:T(8,128)(2,1)S(1)} %copy.39), channel_id=2, replica_groups=mesh['fsdp'=16,'exp'=8] {'fsdp'}, dimensions={0}, use_global_device_ids=true | all-gather | bytes 9248 | tf_op jit(solution)/shard_map/all_gather | solution.py:52
  130.7 0.1 reshape.110
  130.8 109.5 %all-gather.4.cloned.1.call-done = bf16[128,34,3584]{2,0,1:T(8,128)(2,1)} async-done(((bf16[8,34,3584]{2,0,1:T(8,128)(2,1)}), bf16[128,34,3584]{2,0,1:T(8,128)(2,1)}) %all-gather.4.cloned.1.call-update) | async-done | bytes 31195152 | tf_op jit(solution)/shard_map/all_gather | solution.py:51
  240.3 23.6 %copy.41 = bf16[128,34,3584]{2,1,0:T(8,128)(2,1)} copy(bf16[128,34,3584]{2,0,1:T(8,128)(2,1)} %all-gather.4.cloned.1.call-done) | data formatting | bytes 62390272 | tf_op jit(solution)/shard_map/all_gather | solution.py:51
  263.9 37.5 %reshape.104 = bf16[4352,3584]{1,0:T(8,128)(2,1)} reshape(bf16[128,34,3584]{2,1,0:T(8,128)(2,1)} %copy.41) | data formatting | bytes 62390272 | tf_op jit(solution)/shard_map/reshape | solution.py:57
  301.4 22.3 %fusion.8 = (bf16[4352,152]{0,1:T(8,128)(2,1)S(1)}, bf16[4352,152]{0,1:T(8,128)(2,1)S(1)}) fusion(bf16[4352,2,152]{0,2,1:T(8,128)(2,1)} %bitcast.82, bf16[4352,3584]{1,0:T(8,128)(2,1)} %reshape.104, bf16[3584,3,152]{0,2,1:T(8,128)(2,1)} %bitcast.81, f32[4352]{0:T(1024)S(1)} %reshape.110), kind=kOutput, calls=%fused_computation.26 | convolution fusion | flops 4752244736 | bytes 37594112 | tf_op jit(solution)/shard_map/dot_general | solution.py:59
  323.7 1.0 copy-done
  324.7 20.3 %convolution_convert_fusion = bf16[4352,3584]{1,0:T(8,128)(2,1)} fusion(bf16[3584,304]{0,1:T(8,128)(2,1)S(1)} %bitcast.79, bf16[4352,152]{0,1:T(8,128)(2,1)S(1)} %get-tuple-element.3, bf16[4352,152]{0,1:T(8,128)(2,1)S(1)} %get-tuple-element.2), kind=kOutput, calls=%fused_computation.8 | convolution fusion | flops 9504210944 | bytes 36020224 | tf_op jit(solution)/shard_map/dot_general | solution.py:66
  345.0 82.6 %all-gather.6.cloned.1.call-done = bf16[128,34,3584]{2,0,1:T(8,128)(2,1)} async-done(((bf16[8,34,3584]{2,0,1:T(8,128)(2,1)}), bf16[128,34,3584]{2,0,1:T(8,128)(2,1)}) %all-gather.6.cloned.1.call-update) | async-done | bytes 31195152 | tf_op jit(solution)/shard_map/all_gather | solution.py:50
  427.6 23.4 %copy.43 = bf16[128,34,3584]{2,1,0:T(8,128)(2,1)} copy(bf16[128,34,3584]{2,0,1:T(8,128)(2,1)} %all-gather.6.cloned.1.call-done) | data formatting | bytes 62390272 | tf_op jit(solution)/shard_map/all_gather | solution.py:50
  451.0 37.7 %reshape.180 = bf16[4352,3584,1]{1,0,2:T(8,128)(2,1)} reshape(bf16[128,34,3584]{2,1,0:T(8,128)(2,1)} %copy.43) | data formatting | bytes 62390272 | tf_op jit(solution)/shard_map/reshape | solution.py:78
  488.7 0.2 pad_maximum_fusion.1
  488.9 15.8 %fusion = bf16[1,3584,2,152]{1,3,2,0:T(8,128)(2,1)S(1)} fusion(bf16[4352,3584,1]{1,0,2:T(8,128)(2,1)} %reshape.180, bf16[2,152,4352]{2,1,0:T(8,128)(2,1)S(1)} %bitcast.78), kind=kOutput, calls=%fused_computation.11 | convolution fusion | flops 9484410880 | bytes 36020224 | tf_op jit(solution)/shard_map/dot_general | solution.py:17
  504.7 110.2 %reduce-scatter.4.cloned.1.call-done = bf16[272,3584]{1,0:T(8,128)(2,1)} async-done(((bf16[4352,3584]{1,0:T(8,128)(2,1)}), bf16[272,3584]{1,0:T(8,128)(2,1)}) %reduce-scatter.4.cloned.1.call-update) | async-done | bytes 1949712
  614.9 2.9 reshape.106
  617.8 5.3 all-to-all-start.2
  623.1 15.6 %fusion.1 = bf16[1,3584,1,152]{1,3,2,0:T(8,128)(2,1)S(1)} fusion(bf16[4352,3584]{1,0:T(8,128)(2,1)} %reshape.104, f32[4352]{0:T(1024)S(1)} %reshape.110, bf16[4352,2,152]{0,2,1:T(8,128)(2,1)} %bitcast.83), kind=kOutput, calls=%fused_computation.13 | convolution fusion | flops 4748158976 | bytes 34948096 | tf_op jit(solution)/shard_map/dot_general | solution.py:17
  638.7 2.0 pad_maximum_fusion
  640.7 10.9 %all-to-all-done.2 = bf16[8,34,3584]{2,1,0:T(8,128)(2,1)} async-done(((bf16[8,34,3584]{2,1,0:T(8,128)(2,1)}), bf16[8,34,3584]{2,1,0:T(8,128)(2,1)}, u32[]{:S(2)}, u32[]{:S(2)}) %all-to-all-start.2) | async-done | bytes 1949728 | tf_op jit(solution)/shard_map/all_to_all | solution.py:74
  651.6 1.9 reshape.107
  653.5 1.1 gather_fusion.1
  654.6 2.0 gather_fusion
  656.7 2.3 add_convert_fusion
  (22 shorter events, 0.2 us)
Async XLA Ops:
  7.2 6.2 copy-start.2
  7.2 233.1 %all-gather.4.cloned.1.call-start = ((), (), s32[]{:S(2)}) async-start(), calls=%async_computation.5 | async-start | bytes 33144832 | tf_op jit(solution)/shard_map/all_gather | solution.py:51
  53.5 1.9 copy-start.3
  55.3 372.3 %all-gather.6.cloned.1.call-start = ((), (), s32[]{:S(2)}) async-start(), calls=%async_computation.6 | async-start | bytes 33144832 | tf_op jit(solution)/shard_map/all_gather | solution.py:50
  96.2 1.9 copy-start.4
  101.5 8.6 %all-to-all-start = ((bf16[8,1,34]{2,1,0:T(2,128)(2,1)}), bf16[8,1,34]{2,1,0:T(2,128)(2,1)S(1)}, u32[]{:S(2)}, u32[]{:S(2)}) async-start(bf16[8,1,34]{2,1,0:T(2,128)(2,1)} %all_to_all.23), calls=%async_computation | async-start | bytes 8192 | tf_op jit(solution)/shard_map/all_to_all | solution.py:45
  105.6 509.3 %reduce-scatter.4.cloned.1.call-start = ((), (), s32[]{:S(2)}) async-start(), calls=%async_computation.7 | async-start | bytes 33144832
  323.7 1.0 copy-start
  451.0 37.7 %copy-start.1 = (bf16[4352,152]{0,1:T(8,128)(2,1)S(1)}, bf16[4352,152]{0,1:T(8,128)(2,1)}, u32[]{:S(2)}) copy-start(bf16[4352,152]{0,1:T(8,128)(2,1)} %copy-done) | copy-start | bytes 3969028
  617.8 33.8 %all-to-all-start.2 = ((bf16[8,34,3584]{2,1,0:T(8,128)(2,1)}), bf16[8,34,3584]{2,1,0:T(8,128)(2,1)}, u32[]{:S(2)}, u32[]{:S(2)}) async-start(bf16[8,34,3584]{2,1,0:T(8,128)(2,1)} %reshape.106), calls=%async_computation.2 | async-start | bytes 4587520 | tf_op jit(solution)/shard_map/all_to_all | solution.py:74
Sparse Core Ops, SparseCore 0:
  55.5 184.7 all-gather.3
  243.0 184.6 all-gather.5
  431.2 183.7 reduce-scatter.3
where the time goes:
time: 676 us; the launch traced here: 666 us
  waiting for transfers between devices  316 us (47%)
  local copies, waits for them, and re-layouts  156 us (23%)
  blocking collectives  89.8 us (13%)
  matrix products  73.9 us (11%)
  between operations  14.2 us (2%)
  starting transfers between devices  9.53 us (1%)
    unnamed x4, waiting for transfers between devices  110 us
    all_gather x1, waiting for transfers between devices, on_device(): lax.all_gather(got_dy, 'fsdp', axis=0, tiled=True)  109 us
    all_gather x1, waiting for transfers between devices, on_device(): lax.all_gather(got_x, 'fsdp', axis=0, tiled=True)  82.6 us
    reshape x1, local copies, waits for them, and re-layouts, on_device(): xs = all_x.reshape(-1, width)  37.7 us
    reshape x1, local copies, waits for them, and re-layouts, on_device(): dys = all_dy.reshape(-1, width)  37.5 us
    all_to_all x1, blocking collectives, on_device(): lax.all_to_all(dy_buf.reshape(experts, capacity, width), 'exp', split_axi...  35.5 us
    all_to_all x1, blocking collectives, on_device(): lax.all_to_all(x_buf.reshape(experts, capacity, width), 'exp', split_axis...  33.7 us
    dot_general x2, matrix products, contract_rows(): lax.dot_general(left, right, (((0,), (0,)), ((), ())), preferred_element_...  31.4 us
  transfers between devices with their start and end apart: 5, of which 5 were waited for; matrix products, arithmetic and copies ran while one was open for 32% of the time, Pallas kernels for 0%

commit v1 on v0

v1 whole, which is shorter than its diff:
```python
import functools

import jax
import jax.numpy as jnp
import numpy as np
from jax import lax
from jax.experimental import pallas as pl
from jax.experimental.pallas import tpu as pltpu
from jax.sharding import PartitionSpec as P

MESH = pl.DeviceIdType.MESH
BF16 = jnp.bfloat16
F32 = jnp.float32
SIDE = 4
N_COPIES = 80


def round_up(value, unit):
    return -(-value // unit) * unit


def chunk_of(width):
    return 512 if width % 512 == 0 else 128


def dot(left, right, dims):
    return lax.dot_general(left, right, (dims, ((), ())), preferred_element_type=F32)


def rows_of(start, size):
    return pl.ds(pl.multiple_of(start, 16), size)


def cols_of(start, size):
    return pl.ds(pl.multiple_of(start, 128), size)


def kernel(
    cap,
    capp,
    ids_ref,
    probs_ref,
    tok_ref,
    gout_ref,
    pack_ref,
    unpack_ref,
    w_hbm,
    w2_hbm,
    pre_hbm,
    gt_ref,
    dw_hbm,
    g_buf,
    x_buf,
    w13,
    w2,
    pre,
    dgt,
    dg,
    sct,
    acc,
    asend,
    arecv,
    dxr,
    sxt,
    send_sem,
    recv_sem,
    local_sem,
    credit_a,
    credit_b,
    credit_z,
):
    f = lax.axis_index("fsdp")
    e = lax.axis_index("exp")
    experts = lax.axis_size("exp")
    q, p = f // SIDE, f % SIDE
    tokens, width = tok_ref.shape
    half = width // 2
    low, high = pl.ds(0, half), pl.ds(half, half)
    nc = chunk_of(width)
    steps = width // nc
    slots = experts * capp
    rb = experts * cap
    rows = SIDE * rb
    rp = g_buf.shape[0]
    h2 = w13.shape[0] // SIDE
    h = h2 // 2
    hp = w2.shape[0] // SIDE
    shift = (rows * q) % 128

    def dev_p(d):
        return (SIDE * q + (p + d) % SIDE, e)

    def dev_q(d):
        return (SIDE * ((q + d) % SIDE) + p, e)

    def dev_e(d):
        return (f, (e + d) % experts)

    count = [0]

    def rcopy(src, dst, dev):
        i = count[0]
        count[0] += 1
        c = pltpu.make_async_remote_copy(
            src_ref=src,
            dst_ref=dst,
            send_sem=send_sem.at[i],
            recv_sem=recv_sem.at[i],
            device_id=dev,
            device_id_type=MESH,
        )
        c.start()
        return c

    barrier = pltpu.get_barrier_semaphore()
    peers = [dev_p(1), dev_p(3), dev_q(1), dev_q(2), dev_q(3)]
    peers += [dev_e(d) for d in range(1, experts)]
    for dev in peers:
        pl.semaphore_signal(barrier, inc=1, device_id=dev, device_id_type=MESH)
    pl.semaphore_wait(barrier, len(peers))

    def pre_cols(to):
        return cols_of((rows * to) // 128 * 128, rp)

    my_pre = pl.ds(pl.multiple_of(q * rp, 128), rp)
    w13_src = w_hbm.at[pl.ds(0, h2)]

    def ring_start(src, buf, off, pos, dev):
        mine = buf.at[off(pos)]
        return [rcopy(src, mine, dev(1)), rcopy(src, mine, dev(3))]

    def ring_forward(first, buf, off, pos, dev):
        first[0].wait_recv()
        part = buf.at[off((pos + 3) % SIDE), low]
        up = rcopy(part, part, dev(1))
        first[1].wait_recv()
        part = buf.at[off((pos + 1) % SIDE), high]
        down = rcopy(part, part, dev(3))
        return [up, down]

    def wait_recv(copies):
        for c in copies:
            c.wait_recv()

    def wait_send(copies):
        for c in copies:
            c.wait_send()

    w2_off = lambda j: rows_of(hp * j, hp)
    w13_off = lambda j: rows_of(h2 * j, h2)
    row_off = lambda b: rows_of(shift + rb * b, rb)

    w2_copies = ring_start(w2_hbm, w2, w2_off, q, dev_q)
    pre_copies = [
        rcopy(pre_hbm.at[:, pre_cols((q + d) % SIDE)], pre.at[:, my_pre], dev_q(d))
        for d in (1, 2, 3)
    ]
    w13_copies = ring_start(w13_src, w13, w13_off, q, dev_q)
    local = [
        pltpu.make_async_copy(w2_hbm, w2.at[w2_off(q)], local_sem.at[0]),
        pltpu.make_async_copy(pre_hbm.at[:, pre_cols(q)], pre.at[:, my_pre], local_sem.at[1]),
        pltpu.make_async_copy(w13_src, w13.at[w13_off(q)], local_sem.at[2]),
    ]
    for c in local:
        c.start()

    ids = ids_ref[...]
    probs = probs_ref[...].astype(F32)
    kinds = lax.broadcasted_iota(jnp.int32, (experts, tokens), 0)
    hit = [(kinds == ids[k : k + 1, :]).astype(F32) for k in (0, 1)]
    earlier = (
        lax.broadcasted_iota(jnp.int32, (tokens, tokens), 0)
        < lax.broadcasted_iota(jnp.int32, (tokens, tokens), 1)
    ).astype(BF16)
    before = dot((hit[0] + hit[1]).astype(BF16), earlier, ((1,), (0,)))
    place = lax.broadcasted_iota(jnp.int32, (slots, tokens), 0)
    chosen = []
    for k in (0, 1):
        slot = jnp.sum(before * hit[k], axis=0, keepdims=True).astype(jnp.int32)
        chosen.append((place == ids[k : k + 1, :] * capp + slot).astype(F32))
    pick = chosen[0] + chosen[1]
    sxt[...] = jnp.transpose(pick).astype(BF16)
    pick_g = (chosen[0] * probs[0:1, :] + chosen[1] * probs[1:2, :]).astype(BF16)
    pick_x = pick.astype(BF16)

    def exchange(base, copies_from, dst_base):
        copies = []
        for d in range(1, experts):
            src = copies_from.at[rows_of(base + capp * ((e + d) % experts), capp)]
            dst = arecv.at[rows_of(dst_base + capp * e, capp)]
            copies.append(rcopy(src, dst, dev_e(d)))
        return copies

    def dispatch(base, matrix, source):
        def body(n, _):
            cols = cols_of(n * nc, nc)
            asend[pl.ds(base, slots), cols] = dot(
                matrix, source[:, cols], ((1,), (0,))
            ).astype(BF16)
            return 0

        lax.fori_loop(0, steps, body, 0)
        return exchange(base, asend, base)

    g_sent = dispatch(0, pick_g, gout_ref)
    x_sent = dispatch(slots, pick_x, tok_ref)

    blank = rows_of(rows * (1 - q % 2), rp - rows)
    g_buf[blank, :] = jnp.zeros((rp - rows, width), BF16)
    x_buf[blank, :] = jnp.zeros((rp - rows, width), BF16)

    def compact(base, buf):
        own = rows_of(base + capp * e, capp)
        arecv[own, :] = asend[own, :]

        def body(n, _):
            cols = cols_of(n * nc, nc)
            buf[row_off(p), cols] = dot(
                pack_ref[...], arecv[pl.ds(base, slots), cols], ((1,), (0,))
            ).astype(BF16)
            return 0

        lax.fori_loop(0, steps, body, 0)

    wait_recv(g_sent)
    compact(0, g_buf)
    g_copies = ring_start(g_buf.at[row_off(p)], g_buf, row_off, p, dev_p)
    for d in range(1, experts):
        pl.semaphore_signal(credit_z, inc=1, device_id=dev_e(d), device_id_type=MESH)
    wait_recv(x_sent)
    compact(slots, x_buf)
    x_copies = ring_start(x_buf.at[row_off(p)], x_buf, row_off, p, dev_p)

    w2_copies += ring_forward(w2_copies, w2, w2_off, q, dev_q)
    g_copies += ring_forward(g_copies, g_buf, row_off, p, dev_p)
    for c in local:
        c.wait()
    wait_recv(w2_copies[2:])
    w13_copies += ring_forward(w13_copies, w13, w13_off, q, dev_q)
    wait_recv(g_copies[2:])

    acc[...] = jnp.zeros_like(acc)

    def back_step(n, _):
        cols = cols_of(n * nc, nc)
        acc[...] += dot(w2[:, cols], g_buf[:, cols], ((1,), (1,)))
        return 0

    lax.fori_loop(0, steps, back_step, 0)
    x_copies += ring_forward(x_copies, x_buf, row_off, p, dev_p)
    wait_recv(pre_copies)

    def activate(i, _):
        j, c = i // (rp // 128), i % (rp // 128)
        lanes = cols_of(c * 128, 128)
        saved = pre[:, cols_of(j * rp + c * 128, 128)].astype(F32)
        back = acc[rows_of(hp * j, hp), lanes][:h]
        a, b = saved[:h], saved[h:]
        sig = jax.nn.sigmoid(a)
        act = a * sig
        d_gate = back * b * sig * (1.0 + a * (1.0 - sig))
        d_up = back * act
        dgt[rows_of(h2 * j, h2), lanes] = jnp.concatenate([d_gate, d_up], 0).astype(BF16)
        scaled = jnp.concatenate([act * b, jnp.zeros((hp - h, 128), F32)], 0)
        sct[rows_of(hp * j, hp), lanes] = scaled.astype(BF16)
        return 0

    lax.fori_loop(0, SIDE * (rp // 128), activate, 0)

    wait_send(w2_copies)
    for d in (1, 3):
        pl.semaphore_signal(credit_a, inc=1, device_id=dev_q(d), device_id_type=MESH)

    def send_far(part, off, pos, dst, dev):
        far = off((pos + 2) % SIDE)
        return [
            rcopy(part.at[far, low], dst.at[:, low], dev(1)),
            rcopy(part.at[far, high], dst.at[:, high], dev(3)),
        ]

    def send_near_direct(part, off, pos, dst, dev):
        return [
            rcopy(part.at[off((pos + 1) % SIDE), high], dst[0].at[:, high], dev(1)),
            rcopy(part.at[off((pos + 3) % SIDE), low], dst[1].at[:, low], dev(3)),
        ]

    def add_into(part, where, others, start, size):
        ac = 256 if half % 256 == 0 else 128

        def body(n, _):
            cols = cols_of(start + n * ac, ac)
            total = part[where, cols].astype(F32)
            for ref in others:
                total = total + ref[:, cols].astype(F32)
            part[where, cols] = total.astype(BF16)
            return 0

        lax.fori_loop(0, size // ac, body, 0)

    def send_near_added(far, part, off, pos, got, dst, dev):
        far[0].wait_recv()
        where = off((pos + 1) % SIDE)
        add_into(part, where, [got], 0, half)
        up = rcopy(part.at[where, low], dst[0].at[:, low], dev(1))
        far[1].wait_recv()
        where = off((pos + 3) % SIDE)
        add_into(part, where, [got], half, half)
        down = rcopy(part.at[where, high], dst[1].at[:, high], dev(3))
        return [up, down]

    wait_send(g_sent)
    wait_send(x_sent)

    def dw2_step(n, _):
        cols = cols_of(n * nc, nc)
        asend[pl.ds(0, SIDE * hp), cols] = dot(sct[...], g_buf[:, cols], ((1,), (0,))).astype(BF16)
        return 0

    lax.fori_loop(0, steps, dw2_step, 0)
    pl.semaphore_wait(credit_a, 2)
    dw2_near = [w2.at[pl.ds(hp, hp)], w2.at[pl.ds(2 * hp, hp)]]
    dw2_far_got = w2.at[pl.ds(0, hp)]
    dw2_far = send_far(asend, w2_off, q, dw2_far_got, dev_q)
    dw2_mid = send_near_direct(asend, w2_off, q, dw2_near, dev_q)

    def flip(c, _):
        lanes = cols_of(c * 128, 128)
        dg[rows_of(c * 128, 128), :] = jnp.transpose(dgt[:, lanes])
        return 0

    lax.fori_loop(0, rp // 128, flip, 0)

    wait_send(g_copies)
    wait_recv(w13_copies[2:])
    dx_off = lambda b: rows_of(rb * b, rb)

    def dx_block(d):
        b = (p + d) % SIDE

        def body(n, _):
            cols = cols_of(n * nc, nc)
            g_buf[dx_off(b), cols] = dot(dg[row_off(b), :], w13[:, cols], ((1,), (0,))).astype(BF16)
            return 0

        lax.fori_loop(0, steps, body, 0)

    dx_far_got = dxr.at[pl.ds(0, rb)]
    dx_near = [dxr.at[pl.ds(rb, rb)], dxr.at[pl.ds(2 * rb, rb)]]
    dx_block(2)
    dx_far = send_far(g_buf, dx_off, p, dx_far_got, dev_p)
    dx_block(1)
    dx_block(3)
    dx_mid = send_near_direct(g_buf, dx_off, p, dx_near, dev_p)
    dx_block(0)
    dw2_mid += send_near_added(dw2_far, asend, w2_off, q, dw2_far_got, dw2_near, dev_q)
    dx_mid += send_near_added(dx_far, g_buf, dx_off, p, dx_far_got, dx_near, dev_p)

    wait_send(w13_copies)
    wait_recv(x_copies[2:])

    def dw13_block(d):
        j = (q + d) % SIDE

        def body(n, _):
            cols = cols_of(n * nc, nc)
            w13[w13_off(j), cols] = dot(
                dgt[w13_off(j), :], x_buf[:, cols], ((1,), (0,))
            ).astype(BF16)
            return 0

        lax.fori_loop(0, steps, body, 0)

    dw13_far_got = pre.at[:, pl.ds(0, width)]
    dw13_near = [x_buf.at[pl.ds(0, h2)], x_buf.at[pl.ds(h2, h2)]]
    dw13_block(2)
    dw13_far = send_far(w13, w13_off, q, dw13_far_got, dev_q)
    dw13_block(1)
    dw13_block(3)
    dw13_block(0)
    wait_send(x_copies)
    for d in (1, 3):
        pl.semaphore_signal(credit_b, inc=1, device_id=dev_q(d), device_id_type=MESH)
    pl.semaphore_wait(credit_b, 2)
    dw13_mid = send_near_direct(w13, w13_off, q, dw13_near, dev_q)
    dw13_mid += send_near_added(dw13_far, w13, w13_off, q, dw13_far_got, dw13_near, dev_q)

    wait_recv(dx_mid)
    add_into(g_buf, dx_off(p), dx_near, 0, width)
    ret_base = slots

    def expand(n, _):
        cols = cols_of(n * nc, nc)
        arecv[pl.ds(ret_base, slots), cols] = dot(
            unpack_ref[...], g_buf[dx_off(p), cols], ((1,), (0,))
        ).astype(BF16)
        return 0

    lax.fori_loop(0, steps, expand, 0)
    pl.semaphore_wait(credit_z, experts - 1)
    ret = exchange(ret_base, arecv, 0)
    arecv[rows_of(capp * e, capp), :] = arecv[rows_of(ret_base + capp * e, capp), :]

    wait_recv(dw2_mid)
    add_into(asend, w2_off(q), dw2_near, 0, width)
    out2 = pltpu.make_async_copy(
        asend.at[w2_off(q)], dw_hbm.at[pl.ds(h2, hp)], local_sem.at[3]
    )
    out2.start()

    wait_recv(ret)

    def combine(n, _):
        cols = cols_of(n * nc, nc)
        gt_ref[:, cols] = dot(sxt[...], arecv[pl.ds(0, slots), cols], ((1,), (0,))).astype(BF16)
        return 0

    lax.fori_loop(0, steps, combine, 0)

    wait_recv(dw13_mid)
    add_into(w13, w13_off(q), dw13_near, 0, width)
    out13 = pltpu.make_async_copy(
        w13.at[w13_off(q)], dw_hbm.at[pl.ds(0, h2)], local_sem.at[4]
    )
    out13.start()

    wait_send(pre_copies)
    wait_send(dw2_far + dw2_mid + dx_far + dx_mid + dw13_far + dw13_mid + ret)
    out2.wait()
    out13.wait()


def on_device(tokens, grad_out, route_probs, expert_ids, saved_pre, expert_weights):
    rows, width = tokens.shape
    experts = lax.axis_size("exp")
    cap = 17 * rows // (8 * experts)
    capp = round_up(cap, 16)
    slots = experts * capp
    rb = experts * cap
    hidden = expert_weights.shape[3]
    hp = round_up(hidden, 16)
    rp = round_up(SIDE * rb + 64, 128)
    w = jnp.transpose(expert_weights[0], (1, 2, 0)).reshape(3 * hidden, width)
    w2 = jnp.pad(w[2 * hidden :], ((0, hp - hidden), (0, 0)))
    pre = jnp.transpose(saved_pre[0], (1, 2, 0)).reshape(2 * hidden, saved_pre.shape[1])
    at = np.arange(rb)
    pack = np.zeros((rb, slots), np.float32)
    pack[at, at // cap * capp + at % cap] = 1
    vmem = pl.BlockSpec(memory_space=pltpu.VMEM)
    hbm = pl.BlockSpec(memory_space=pl.ANY)
    gt, dw = pl.pallas_call(
        functools.partial(kernel, cap, capp),
        out_shape=(
            jax.ShapeDtypeStruct((rows, width), BF16),
            jax.ShapeDtypeStruct((2 * hidden + hp, width), BF16),
        ),
        in_specs=[vmem] * 6 + [hbm] * 3,
        out_specs=(vmem, hbm),
        scratch_shapes=[
            pltpu.VMEM((rp, width), BF16),
            pltpu.VMEM((rp, width), BF16),
            pltpu.VMEM((SIDE * 2 * hidden, width), BF16),
            pltpu.VMEM((SIDE * hp, width), BF16),
            pltpu.VMEM((2 * hidden, SIDE * rp), BF16),
            pltpu.VMEM((SIDE * 2 * hidden, rp), BF16),
            pltpu.VMEM((rp, SIDE * 2 * hidden), BF16),
            pltpu.VMEM((SIDE * hp, rp), BF16),
            pltpu.VMEM((SIDE * hp, rp), F32),
            pltpu.VMEM((max(2 * slots, SIDE * hp), width), BF16),
            pltpu.VMEM((2 * slots, width), BF16),
            pltpu.VMEM((3 * rb, width), BF16),
            pltpu.VMEM((rows, slots), BF16),
            pltpu.SemaphoreType.DMA((N_COPIES,)),
            pltpu.SemaphoreType.DMA((N_COPIES,)),
            pltpu.SemaphoreType.DMA((5,)),
            pltpu.SemaphoreType.REGULAR,
            pltpu.SemaphoreType.REGULAR,
            pltpu.SemaphoreType.REGULAR,
        ],
        compiler_params=pltpu.CompilerParams(
            collective_id=0, has_side_effects=True, vmem_limit_bytes=64 * 2**20
        ),
        name="experts_backward",
    )(
        expert_ids.T,
        route_probs.T,
        tokens,
        grad_out,
        jnp.asarray(pack, BF16),
        jnp.asarray(pack.T, BF16),
        w,
        w2,
        pre,
    )
    grad = dw[: 3 * hidden].reshape(3, hidden, width)
    return gt, jnp.transpose(grad, (2, 0, 1))[None]


def solution(mesh):
    in_specs = (
        P(("fsdp", "exp"), None),
        P(("fsdp", "exp"), None),
        P(("fsdp", "exp"), None),
        P(("fsdp", "exp"), None),
        P("exp", None, None, "fsdp"),
        P("exp", None, None, "fsdp"),
    )
    out_specs = (P(("fsdp", "exp"), None), P("exp", None, None, "fsdp"))
    return jax.shard_map(
        on_device, mesh=mesh, in_specs=in_specs, out_specs=out_specs, check_vma=False
    )
```

time: 676 us -> 279 us (0.41); the launches traced: 666 us -> 279 us
  waiting for transfers between devices: 316 us -> 0 us
  Pallas kernels: 0 us -> 271 us
  local copies, waits for them, and re-layouts: 156 us -> 7.24 us
  blocking collectives: 89.8 us -> 0 us
  matrix products: 73.9 us -> 0 us
  between operations: 14.2 us -> 0.65 us
  starting transfers between devices: 9.53 us -> 0 us
    pallas_call x0 -> x1, Pallas kernels: none -> 271 us  [on_device(): pl.pallas_call(functools.partial(kernel, cap, capp), out_shape=(jax.Shape...]
    all_gather x2 -> x0, waiting for transfers between devices: 192 us -> none  [the longest x1 109 us: on_device(): lax.all_gather(got_dy, 'fsdp', axis=0, tiled=True)]
    unnamed x4 -> x0, waiting for transfers between devices: 110 us -> none
    reshape x6 -> x0, local copies, waits for them, and re-layouts: 83.3 us -> none  [the longest x1 37.7 us: on_device(): xs = all_x.reshape(-1, width)]
    dot_general x4 -> x0, matrix products: 73.9 us -> none  [the longest x2 31.4 us: contract_rows(): lax.dot_general(left, right, (((0,), (0,)), ((), ())), preferred_element_...]
    all_to_all x2 -> x0, blocking collectives: 69.3 us -> none  [the longest x1 35.5 us: on_device(): lax.all_to_all(dy_buf.reshape(experts, capacity, width), 'exp', split_axi...]
    all_gather x2 -> x0, local copies, waits for them, and re-layouts: 47 us -> none  [the longest x1 23.6 us: on_device(): lax.all_gather(got_dy, 'fsdp', axis=0, tiled=True)]
    all_gather x1 -> x0, blocking collectives: 20.5 us -> none  [on_device(): lax.all_gather(got_p, 'fsdp', axis=0, tiled=True)]
  transfers between devices with their start and end apart: 5 -> 0, of which waited for: 5 -> 0; matrix products, arithmetic and copies ran while one was open for 32% -> 0% of each run, Pallas kernels for 0% -> 0%
where the time goes in v1:
time: 279 us
  Pallas kernels  271 us (97%)
  local copies, waits for them, and re-layouts  7.24 us (3%)
    pallas_call x1, Pallas kernels, on_device(): pl.pallas_call(functools.partial(kernel, cap, capp), out_shape=(jax.Shape...  271 us

profile of v1, /device:TPU:1, one launch (start us, length us, event | category | flops | bytes accessed | tf_op | source)
XLA Modules:
  0.0 278.7 jit_solution(17730898968527840377)
XLA Ops:
  0.6 1.3 slice_bitcast_fusion
  1.9 1.1 pad.4.w2_hbm
  3.0 270.8 %experts_backward.1 = (bf16[128,3584]{1,0:T(8,128)(2,1)}, bf16[464,3584]{1,0:T(8,128)(2,1)}) custom-call(s32[2,128]{1,0:T(2,128)} %bitcast.23, bf16[2,128]{1,0:T(2,128)(2,1)} %bitcast.24, bf16[128,3584]{1,0:T(8,128)(2,1)} %tok_ref.1, bf16[128,3584]{1,0:T(8,128)(2,1)} %gout_ref.1, bf16[272,384]{1,0:T(8,128)(2,1)} %constant.7.clone.pack_ref, ...), custom_call_target="tpu_custom_call" | custom-call | tf_op jit(solution)/shard_map/experts_backward/pallas_call | solution.py:450
  273.9 0.0 copy-start
  273.9 3.9 %slice.11 = bf16[456,3584]{1,0:T(8,128)(2,1)} slice(bf16[464,3584]{1,0:T(8,128)(2,1)} %get-tuple-element.5), slice={[0:456], [0:3584]} | slice | bytes 6537216 | tf_op jit(solution)/shard_map/slice | solution.py:494
  277.8 0.0 copy-done
  277.8 0.9 copy.11
Async XLA Ops:
  273.9 3.9 %copy-start = (bf16[128,3584]{1,0:T(8,128)(2,1)S(1)}, bf16[128,3584]{1,0:T(8,128)(2,1)}, u32[]{:S(2)}) copy-start(bf16[128,3584]{1,0:T(8,128)(2,1)} %get-tuple-element.8) | copy-start | bytes 2752516

commit v2 on v1

v2 whole, which is shorter than its diff:
```python
import functools

import jax
import jax.numpy as jnp
import numpy as np
from jax import lax
from jax.experimental import pallas as pl
from jax.experimental.pallas import tpu as pltpu
from jax.sharding import PartitionSpec as P

MESH = pl.DeviceIdType.MESH
BF16 = jnp.bfloat16
F32 = jnp.float32
SIDE = 4
N_COPIES = 128


def round_up(value, unit):
    return -(-value // unit) * unit


def chunk_of(width):
    return 512 if width % 512 == 0 else 128


def dot(left, right, dims):
    return lax.dot_general(left, right, (dims, ((), ())), preferred_element_type=F32)


def rows_of(start, size):
    return pl.ds(pl.multiple_of(start, 16), size)


def cols_of(start, size):
    return pl.ds(pl.multiple_of(start, 128), size)


def kernel(
    cap,
    pieces,
    ids_ref,
    probs_ref,
    gout_ref,
    tok_ref,
    lmap_ref,
    fold_ref,
    unfold_ref,
    w_hbm,
    w2_hbm,
    pre_hbm,
    gt_ref,
    dw_hbm,
    g_buf,
    x_buf,
    w13,
    w2,
    pre,
    dgt,
    dg,
    sct,
    acc,
    stage,
    gmain,
    dxr,
    gext,
    gext_got,
    rext,
    rext_got,
    xext,
    xext_got,
    home,
    home_ext,
    send_sem,
    recv_sem,
    local_sem,
    credit_a,
    credit_b,
    credit_z,
):
    f = lax.axis_index("fsdp")
    e = lax.axis_index("exp")
    experts = lax.axis_size("exp")
    core = e % 2
    q = core * (f % SIDE) + (1 - core) * (f // SIDE)
    p = core * (f // SIDE) + (1 - core) * (f % SIDE)
    tokens, width = gout_ref.shape
    half = width // 2
    low, high = pl.ds(0, half), pl.ds(half, half)
    nc = chunk_of(width)
    steps = width // nc
    mb = cap // 16 * 16
    xb = cap - mb
    main = experts * mb
    rb = experts * cap
    rows = SIDE * rb
    rp = g_buf.shape[0]
    h2 = w13.shape[0] // SIDE
    h = h2 // 2
    hp = w2.shape[0] // SIDE
    piece = width // pieces

    def dev_at(pp, qq):
        return (SIDE * (core * pp + (1 - core) * qq) + core * qq + (1 - core) * pp, e)

    def dev_p(d):
        return dev_at((p + d) % SIDE, q)

    def dev_q(d):
        return dev_at(p, (q + d) % SIDE)

    def dev_e(d):
        return (f, (e + d) % experts)

    count = [0]

    def rcopy(src, dst, dev):
        i = count[0]
        count[0] += 1
        c = pltpu.make_async_remote_copy(
            src_ref=src,
            dst_ref=dst,
            send_sem=send_sem.at[i],
            recv_sem=recv_sem.at[i],
            device_id=dev,
            device_id_type=MESH,
        )
        c.start()
        return c

    def signal(sem, devs):
        for dev in devs:
            pl.semaphore_signal(sem, inc=1, device_id=dev, device_id_type=MESH)

    barrier = pltpu.get_barrier_semaphore()
    peers = [dev_p(d) for d in (1, 2, 3)] + [dev_q(d) for d in (1, 2, 3)]
    peers += [dev_e(d) for d in range(1, experts)]
    signal(barrier, peers)
    pl.semaphore_wait(barrier, len(peers))

    def ring_start(src, buf, off, pos, dev):
        mine = buf.at[off(pos)]
        return [rcopy(src, mine, dev(1)), rcopy(src, mine, dev(3))]

    def ring_forward(first, buf, off, pos, dev):
        first[0].wait_recv()
        part = buf.at[off((pos + 3) % SIDE), low]
        up = rcopy(part, part, dev(1))
        first[1].wait_recv()
        part = buf.at[off((pos + 1) % SIDE), high]
        down = rcopy(part, part, dev(3))
        return [up, down]

    def wait_recv(copies):
        for c in copies:
            c.wait_recv()

    def wait_send(copies):
        for c in copies:
            c.wait_send()

    w2_off = lambda j: rows_of(hp * j, hp)
    w13_off = lambda j: rows_of(h2 * j, h2)
    row_off = lambda b: rows_of(rb * b, rb)
    ext_off = lambda b: rows_of(rb * b + main, 16)
    w13_src = w_hbm.at[pl.ds(0, h2)]
    my_pre = pl.ds(pl.multiple_of(q * rp, 128), rp)

    w2_copies = ring_start(w2_hbm, w2, w2_off, q, dev_q)
    strip = pre_hbm.shape[1] // 2
    local = [
        pltpu.make_async_copy(
            pre_hbm.at[:, pl.ds(i * strip, strip)],
            stage.at[pl.ds(i * h2, h2), pl.ds(0, strip)],
            local_sem.at[i],
        )
        for i in (0, 1)
    ]
    local += [
        pltpu.make_async_copy(w2_hbm, w2.at[w2_off(q)], local_sem.at[2]),
        pltpu.make_async_copy(w13_src, w13.at[w13_off(q)], local_sem.at[3]),
    ]
    for c in local:
        c.start()

    ids = ids_ref[...]
    probs = probs_ref[...].astype(F32)
    kinds = lax.broadcasted_iota(jnp.int32, (experts, tokens), 0)
    hit = [(kinds == ids[k : k + 1, :]).astype(F32) for k in (0, 1)]
    earlier = (
        lax.broadcasted_iota(jnp.int32, (tokens, tokens), 0)
        < lax.broadcasted_iota(jnp.int32, (tokens, tokens), 1)
    ).astype(F32).astype(BF16)
    before = dot((hit[0] + hit[1]).astype(BF16), earlier, ((1,), (0,)))
    at_main, at_ext = [], []
    for k in (0, 1):
        own = ids[k : k + 1, :]
        slot = jnp.sum(before * hit[k], axis=0, keepdims=True).astype(jnp.int32)
        inside = slot < mb
        at_main.append(jnp.where(inside, mb * own + slot, -4096))
        at_ext.append(jnp.where(inside, -4096, 16 * own + pieces * (slot - mb)))

    def one_hot(size, where):
        line = lax.broadcasted_iota(jnp.int32, (size, tokens), 0)
        return [(line == w).astype(F32) for w in where]

    def dispatch(source, weights, big, small):
        pick = one_hot(main, at_main)
        if weights is None:
            home[...] = jnp.transpose(pick[0] + pick[1]).astype(BF16)
            pick = (pick[0] + pick[1]).astype(BF16)
        else:
            pick = (pick[0] * weights[0:1, :] + pick[1] * weights[1:2, :]).astype(BF16)

        def pick_step(n, _):
            cols = cols_of(n * nc, nc)
            big[:, cols] = dot(pick, source[:, cols], ((1,), (0,))).astype(BF16)
            return 0

        lax.fori_loop(0, steps, pick_step, 0)
        folded = jnp.zeros((experts * 16, piece), F32)
        for j in range(pieces):
            pick = one_hot(experts * 16, [w + j for w in at_ext])
            if weights is None:
                pick = pick[0] + pick[1]
                home_ext[pl.ds(j * tokens, tokens), :] = jnp.transpose(pick).astype(BF16)
            else:
                pick = pick[0] * weights[0:1, :] + pick[1] * weights[1:2, :]
            folded += dot(pick.astype(BF16), source[:, pl.ds(j * piece, piece)], ((1,), (0,)))
        small[...] = folded.astype(BF16)

    my_slots = rows_of(rb * p + mb * e, mb)

    def exchange(big, small, buf, small_got):
        copies = []
        for d in range(1, experts):
            to = (e + d) % experts
            there = p if d % 2 == 0 else q
            copies += [
                rcopy(
                    big.at[rows_of(mb * to, mb)],
                    buf.at[rows_of(rb * there + mb * e, mb)],
                    dev_e(d),
                ),
                rcopy(small.at[rows_of(16 * to, 16)], small_got.at[rows_of(16 * e, 16)], dev_e(d)),
            ]
        buf[my_slots, :] = big[rows_of(mb * e, mb), :]
        small_got[rows_of(16 * e, 16), :] = small[rows_of(16 * e, 16), :]
        return copies

    def unfold(buf, small_got):
        for j in range(pieces):
            buf[ext_off(p), pl.ds(j * piece, piece)] = dot(
                unfold_ref[pl.ds(16 * j, 16), :], small_got[...], ((1,), (0,))
            ).astype(BF16)

    xmain = stage.at[pl.ds(2 * h2, main), pl.ds(0, width)]
    dispatch(gout_ref, probs, gmain, gext)
    g_sent = exchange(gmain, gext, g_buf, gext_got)
    dispatch(tok_ref, None, xmain, xext)
    blank = pl.ds(rows, rp - rows)
    g_buf[blank, :] = jnp.zeros((rp - rows, width), BF16)
    x_buf[blank, :] = jnp.zeros((rp - rows, width), BF16)

    local[0].wait()
    local[1].wait()
    span = rp // 3
    line = lax.broadcasted_iota(jnp.int32, (span, span), 0)
    lane = lax.broadcasted_iota(jnp.int32, (span, span), 1)

    def regroup(to, _):
        for n in range(3):
            total = jnp.zeros((h2, span), F32)
            source = lmap_ref[0:1, pl.ds(n * span, span)]
            for b in (n, n + 1):
                block = core * (SIDE * b + to) + (1 - core) * (SIDE * to + b)
                start = rb * (block % 8)
                window = stage[rows_of(block // 8 * h2, h2), cols_of(start // 128 * 128, span)]
                at = lane + (n * span - rb * b)
                match = (at >= 0) & (at < rb) & (line - start % 128 == source)
                total += dot(window, match.astype(F32).astype(BF16), ((1,), (0,)))
            dgt[rows_of(h2 * to, h2), pl.ds(n * span, span)] = total.astype(BF16)
        return 0

    lax.fori_loop(0, SIDE, regroup, 0)
    pre_copies = [
        rcopy(dgt.at[rows_of(h2 * ((q + d) % SIDE), h2)], pre.at[:, my_pre], dev_q(d))
        for d in (1, 2, 3)
    ]
    own_pre = pltpu.make_async_copy(dgt.at[rows_of(h2 * q, h2)], pre.at[:, my_pre], local_sem.at[0])
    own_pre.start()

    w13_copies = ring_start(w13_src, w13, w13_off, q, dev_q)
    w2_copies += ring_forward(w2_copies, w2, w2_off, q, dev_q)

    wait_recv(g_sent)
    unfold(g_buf, gext_got)
    g_copies = ring_start(g_buf.at[row_off(p)], g_buf, row_off, p, dev_p)

    x_sent = exchange(xmain, xext, x_buf, xext_got)
    w13_copies += ring_forward(w13_copies, w13, w13_off, q, dev_q)
    g_copies += ring_forward(g_copies, g_buf, row_off, p, dev_p)
    wait_recv(x_sent)
    unfold(x_buf, xext_got)
    x_copies = ring_start(x_buf.at[row_off(p)], x_buf, row_off, p, dev_p)

    wait_send(g_sent)
    signal(credit_z, [dev_e(d) for d in range(1, experts)])
    local[2].wait()
    local[3].wait()
    wait_recv(w2_copies[2:])
    wait_recv(g_copies[2:])

    acc[...] = jnp.zeros_like(acc)

    def back_step(n, _):
        cols = cols_of(n * nc, nc)
        acc[...] += dot(w2[:, cols], g_buf[:, cols], ((1,), (1,)))
        return 0

    lax.fori_loop(0, steps, back_step, 0)
    x_copies += ring_forward(x_copies, x_buf, row_off, p, dev_p)
    wait_recv(pre_copies)
    wait_send(pre_copies)
    own_pre.wait()

    def activate(i, _):
        j, c = i // (rp // 128), i % (rp // 128)
        lanes = cols_of(c * 128, 128)
        saved = pre[:, cols_of(j * rp + c * 128, 128)].astype(F32)
        back = acc[rows_of(hp * j, hp), lanes][:h]
        a, b = saved[:h], saved[h:]
        sig = jax.nn.sigmoid(a)
        act = a * sig
        d_gate = back * b * sig * (1.0 + a * (1.0 - sig))
        d_up = back * act
        dgt[rows_of(h2 * j, h2), lanes] = jnp.concatenate([d_gate, d_up], 0).astype(BF16)
        scaled = jnp.concatenate([act * b, jnp.zeros((hp - h, 128), F32)], 0)
        sct[rows_of(hp * j, hp), lanes] = scaled.astype(BF16)
        return 0

    lax.fori_loop(0, SIDE * (rp // 128), activate, 0)

    wait_send(w2_copies)
    signal(credit_a, [dev_q(1), dev_q(3)])

    def send_far(part, off, pos, dst, dev):
        far = off((pos + 2) % SIDE)
        return [
            rcopy(part.at[far, low], dst.at[:, low], dev(1)),
            rcopy(part.at[far, high], dst.at[:, high], dev(3)),
        ]

    def send_near_direct(part, off, pos, dst, dev):
        return [
            rcopy(part.at[off((pos + 1) % SIDE), high], dst[0].at[:, high], dev(1)),
            rcopy(part.at[off((pos + 3) % SIDE), low], dst[1].at[:, low], dev(3)),
        ]

    def add_into(part, where, others, start, size):
        ac = 256 if half % 256 == 0 else 128

        def add_step(n, _):
            cols = cols_of(start + n * ac, ac)
            total = part[where, cols].astype(F32)
            for ref in others:
                total = total + ref[:, cols].astype(F32)
            part[where, cols] = total.astype(BF16)
            return 0

        lax.fori_loop(0, size // ac, add_step, 0)

    def send_near_added(far, part, off, pos, got, dst, dev):
        far[0].wait_recv()
        where = off((pos + 1) % SIDE)
        add_into(part, where, [got], 0, half)
        up = rcopy(part.at[where, low], dst[0].at[:, low], dev(1))
        far[1].wait_recv()
        where = off((pos + 3) % SIDE)
        add_into(part, where, [got], half, half)
        down = rcopy(part.at[where, high], dst[1].at[:, high], dev(3))
        return [up, down]

    wait_send(x_sent)

    def dw2_step(n, _):
        cols = cols_of(n * nc, nc)
        stage[pl.ds(0, SIDE * hp), cols] = dot(sct[...], g_buf[:, cols], ((1,), (0,))).astype(BF16)
        return 0

    lax.fori_loop(0, steps, dw2_step, 0)
    pl.semaphore_wait(credit_a, 2)
    dw2_near = [w2.at[pl.ds(hp, hp)], w2.at[pl.ds(2 * hp, hp)]]
    dw2_far_got = w2.at[pl.ds(0, hp)]
    dw2_far = send_far(stage, w2_off, q, dw2_far_got, dev_q)
    dw2_mid = send_near_direct(stage, w2_off, q, dw2_near, dev_q)

    def flip(c, _):
        lanes = cols_of(c * 128, 128)
        dg[rows_of(c * 128, 128), :] = jnp.transpose(dgt[:, lanes])
        return 0

    lax.fori_loop(0, rp // 128, flip, 0)
    dw2_mid += send_near_added(dw2_far, stage, w2_off, q, dw2_far_got, dw2_near, dev_q)

    wait_send(g_copies)
    wait_recv(w13_copies[2:])

    def dx_block(d):
        b = (p + d) % SIDE

        def dx_step(n, _):
            cols = cols_of(n * nc, nc)
            g_buf[row_off(b), cols] = dot(dg[row_off(b), :], w13[:, cols], ((1,), (0,))).astype(BF16)
            return 0

        lax.fori_loop(0, steps, dx_step, 0)

    dx_far_got = dxr.at[pl.ds(0, rb), pl.ds(0, width)]
    dx_near = [dxr.at[pl.ds(rb * i, rb), pl.ds(0, width)] for i in (1, 2)]
    dx_block(2)
    dx_far = send_far(g_buf, row_off, p, dx_far_got, dev_p)
    dx_block(1)
    dx_block(3)
    dx_mid = send_near_direct(g_buf, row_off, p, dx_near, dev_p)
    dx_block(0)
    dx_mid += send_near_added(dx_far, g_buf, row_off, p, dx_far_got, dx_near, dev_p)

    wait_recv(x_copies[2:])
    wait_send(w13_copies)

    def dw13_block(d):
        j = (q + d) % SIDE

        def dw13_step(n, _):
            cols = cols_of(n * nc, nc)
            w13[w13_off(j), cols] = dot(
                dgt[w13_off(j), :], x_buf[:, cols], ((1,), (0,))
            ).astype(BF16)
            return 0

        lax.fori_loop(0, steps, dw13_step, 0)

    dw13_far_got = pre.at[:, pl.ds(0, width)]
    dw13_near = [x_buf.at[pl.ds(0, h2)], x_buf.at[pl.ds(h2, h2)]]
    dw13_block(2)
    dw13_far = send_far(w13, w13_off, q, dw13_far_got, dev_q)
    dw13_block(1)
    dw13_block(3)
    dw13_block(0)
    wait_send(x_copies)
    signal(credit_b, [dev_q(1), dev_q(3)])
    pl.semaphore_wait(credit_b, 2)
    dw13_mid = send_near_direct(w13, w13_off, q, dw13_near, dev_q)
    dw13_mid += send_near_added(dw13_far, w13, w13_off, q, dw13_far_got, dw13_near, dev_q)

    wait_recv(dx_mid)
    add_into(g_buf, row_off(p), dx_near, 0, width)
    folded = jnp.zeros((experts * 16, piece), F32)
    for j in range(pieces):
        folded += dot(
            fold_ref[pl.ds(j * experts * 16, experts * 16), :],
            g_buf[ext_off(p), pl.ds(j * piece, piece)],
            ((1,), (0,)),
        )
    rext[...] = folded.astype(BF16)
    pl.semaphore_wait(credit_z, experts - 1)
    ret = []
    for d in range(1, experts):
        to = (e + d) % experts
        ret.append(
            rcopy(
                g_buf.at[rows_of(rb * p + mb * to, mb)], gmain.at[rows_of(mb * e, mb)], dev_e(d)
            )
        )
        ret.append(
            rcopy(rext.at[rows_of(16 * to, 16)], rext_got.at[rows_of(16 * e, 16)], dev_e(d))
        )
    gmain[rows_of(mb * e, mb), :] = g_buf[my_slots, :]
    rext_got[rows_of(16 * e, 16), :] = rext[rows_of(16 * e, 16), :]

    wait_recv(dw2_mid)
    add_into(stage, w2_off(q), dw2_near, 0, width)
    out2 = pltpu.make_async_copy(
        stage.at[w2_off(q), pl.ds(0, width)], dw_hbm.at[pl.ds(h2, hp)], local_sem.at[0]
    )
    out2.start()

    wait_recv(ret)
    for j in range(pieces):
        cols = pl.ds(j * piece, piece)
        total = dot(home[...], gmain[:, cols], ((1,), (0,)))
        total += dot(home_ext[pl.ds(j * tokens, tokens), :], rext_got[...], ((1,), (0,)))
        gt_ref[:, cols] = total.astype(BF16)

    wait_recv(dw13_mid)
    add_into(w13, w13_off(q), dw13_near, 0, width)
    out13 = pltpu.make_async_copy(w13.at[w13_off(q)], dw_hbm.at[pl.ds(0, h2)], local_sem.at[1])
    out13.start()

    wait_send(dw2_far + dw2_mid + dx_far + dx_mid + dw13_far + dw13_mid + ret)
    out2.wait()
    out13.wait()


def on_device(tokens, grad_out, route_probs, expert_ids, saved_pre, expert_weights):
    rows, width = tokens.shape
    experts = lax.axis_size("exp")
    cap = 17 * rows // (8 * experts)
    mb = cap // 16 * 16
    xb = cap - mb
    main = experts * mb
    rb = experts * cap
    hidden = expert_weights.shape[3]
    hp = round_up(hidden, 16)
    rp = round_up(SIDE * rb + 64, 128)
    strip = saved_pre.shape[1] // 2
    pieces = max(k for k in range(1, 16 // xb + 1) if width % (128 * k) == 0)
    w = jnp.transpose(expert_weights[0], (1, 2, 0)).reshape(3 * hidden, width)
    w2 = lax.pad(w, jnp.zeros((), BF16), ((-2 * hidden, hp - hidden, 0), (0, 0, 0)))
    pre = jnp.transpose(saved_pre[0], (1, 2, 0)).reshape(2 * hidden, saved_pre.shape[1])

    at = np.arange(rb)
    in_main = at // mb * cap + at % mb
    in_ext = (at - main) // xb * cap + mb + (at - main) % xb
    lmap = np.full((8, rp), -1, np.int32)
    lmap[:, : SIDE * rb] = np.tile(np.where(at < main, in_main, in_ext), SIDE)
    ext = np.arange(16)
    unfold = np.zeros((pieces, 16, experts * 16), np.float32)
    for j in range(pieces):
        unfold[j, ext, 16 * (ext // xb) + pieces * (ext % xb) + j] = 1
    fold = unfold.transpose(0, 2, 1).reshape(pieces * experts * 16, 16)
    unfold = unfold.reshape(pieces * 16, experts * 16)

    vmem = pl.BlockSpec(memory_space=pltpu.VMEM)
    hbm = pl.BlockSpec(memory_space=pl.ANY)
    gt, dw = pl.pallas_call(
        functools.partial(kernel, cap, pieces),
        out_shape=(
            jax.ShapeDtypeStruct((rows, width), BF16),
            jax.ShapeDtypeStruct((2 * hidden + hp, width), BF16),
        ),
        in_specs=[vmem] * 7 + [hbm] * 3,
        out_specs=(vmem, hbm),
        scratch_shapes=[
            pltpu.VMEM((rp, width), BF16),
            pltpu.VMEM((rp, width), BF16),
            pltpu.VMEM((SIDE * 2 * hidden, width), BF16),
            pltpu.VMEM((SIDE * hp, width), BF16),
            pltpu.VMEM((2 * hidden, SIDE * rp), BF16),
            pltpu.VMEM((SIDE * 2 * hidden, rp), BF16),
            pltpu.VMEM((rp, SIDE * 2 * hidden), BF16),
            pltpu.VMEM((SIDE * hp, rp), BF16),
            pltpu.VMEM((SIDE * hp, rp), F32),
            pltpu.VMEM((4 * hidden + main, max(width, strip)), BF16),
            pltpu.VMEM((main, width), BF16),
            pltpu.VMEM((3 * rb, width), BF16),
            pltpu.VMEM((experts * 16, width // pieces), BF16),
            pltpu.VMEM((experts * 16, width // pieces), BF16),
            pltpu.VMEM((experts * 16, width // pieces), BF16),
            pltpu.VMEM((experts * 16, width // pieces), BF16),
            pltpu.VMEM((experts * 16, width // pieces), BF16),
            pltpu.VMEM((experts * 16, width // pieces), BF16),
            pltpu.VMEM((rows, main), BF16),
            pltpu.VMEM((pieces * rows, experts * 16), BF16),
            pltpu.SemaphoreType.DMA((N_COPIES,)),
            pltpu.SemaphoreType.DMA((N_COPIES,)),
            pltpu.SemaphoreType.DMA((5,)),
            pltpu.SemaphoreType.REGULAR,
            pltpu.SemaphoreType.REGULAR,
            pltpu.SemaphoreType.REGULAR,
        ],
        compiler_params=pltpu.CompilerParams(
            collective_id=0, has_side_effects=True, vmem_limit_bytes=64 * 2**20
        ),
        name="experts_backward",
    )(
        expert_ids.T,
        route_probs.T,
        grad_out,
        tokens,
        jnp.asarray(lmap),
        jnp.asarray(fold, BF16),
        jnp.asarray(unfold, BF16),
        w,
        w2,
        pre,
    )
    grad = dw[: 3 * hidden].reshape(3, hidden, width)
    return gt, jnp.transpose(grad, (2, 0, 1))[None]


def solution(mesh):
    in_specs = (
        P(("fsdp", "exp"), None),
        P(("fsdp", "exp"), None),
        P(("fsdp", "exp"), None),
        P(("fsdp", "exp"), None),
        P("exp", None, None, "fsdp"),
        P("exp", None, None, "fsdp"),
    )
    out_specs = (P(("fsdp", "exp"), None), P("exp", None, None, "fsdp"))
    return jax.shard_map(
        on_device, mesh=mesh, in_specs=in_specs, out_specs=out_specs, check_vma=False
    )
```

time: 279 us -> 247 us (0.89)
  Pallas kernels: 271 us -> 239 us
    pallas_call x1, Pallas kernels: 271 us -> 239 us  [on_device(): pl.pallas_call(functools.partial(kernel, cap, pieces), out_shape=(jax.Sha...]
where the time goes in v2:
time: 247 us
  Pallas kernels  239 us (97%)
  local copies, waits for them, and re-layouts  7.16 us (3%)
    pallas_call x1, Pallas kernels, on_device(): pl.pallas_call(functools.partial(kernel, cap, pieces), out_shape=(jax.Sha...  239 us

profile of v2, /device:TPU:1, one launch (start us, length us, event | category | flops | bytes accessed | tf_op | source)
XLA Modules:
  0.0 247.2 jit_solution(11539322736269684929)
XLA Ops:
  0.6 2.3 pad_slice_fusion.w2_hbm
  2.9 239.4 %experts_backward.1 = (bf16[128,3584]{1,0:T(8,128)(2,1)}, bf16[464,3584]{1,0:T(8,128)(2,1)}) custom-call(s32[2,128]{1,0:T(2,128)} %bitcast.21, bf16[2,128]{1,0:T(2,128)(2,1)} %bitcast.22, bf16[128,3584]{1,0:T(8,128)(2,1)} %gout_ref.1, bf16[128,3584]{1,0:T(8,128)(2,1)} %tok_ref.1, s32[8,1152]{1,0:T(8,128)} %constant.8.clone.lmap_ref, ...), custom_call_target="tpu_custom_call" | custom-call | tf_op jit(solution)/shard_map/experts_backward/pallas_call | solution.py:536
  242.4 0.0 copy-start
  242.4 3.9 %slice.4 = bf16[456,3584]{1,0:T(8,128)(2,1)} slice(bf16[464,3584]{1,0:T(8,128)(2,1)} %get-tuple-element.5), slice={[0:456], [0:3584]} | slice | bytes 6537216 | tf_op jit(solution)/shard_map/slice | solution.py:588
  246.3 0.0 copy-done
  246.3 0.9 copy.12
Async XLA Ops:
  242.4 3.9 %copy-start = (bf16[128,3584]{1,0:T(8,128)(2,1)S(1)}, bf16[128,3584]{1,0:T(8,128)(2,1)}, u32[]{:S(2)}) copy-start(bf16[128,3584]{1,0:T(8,128)(2,1)} %get-tuple-element.8) | copy-start | bytes 2752516

commit v3 on v2

--- a/solution.py
+++ b/solution.py
@@ -46,7 +46,7 @@
     fold_ref,
     unfold_ref,
     w_hbm,
-    w2_hbm,
+    w3_hbm,
     pre_hbm,
     gt_ref,
     dw_hbm,
@@ -60,6 +60,7 @@
     sct,
     acc,
     stage,
+    xmain,
     gmain,
     dxr,
     gext,
@@ -96,7 +97,7 @@
     rp = g_buf.shape[0]
     h2 = w13.shape[0] // SIDE
     h = h2 // 2
-    hp = w2.shape[0] // SIDE
+    hp = sct.shape[0] // SIDE
     piece = width // pieces
 
     def dev_at(pp, qq):
@@ -137,16 +138,19 @@
     signal(barrier, peers)
     pl.semaphore_wait(barrier, len(peers))
 
+    def view(ref, where, cols):
+        return ref.at[where, :, cols] if len(ref.shape) == 3 else ref.at[where, cols]
+
     def ring_start(src, buf, off, pos, dev):
         mine = buf.at[off(pos)]
         return [rcopy(src, mine, dev(1)), rcopy(src, mine, dev(3))]
 
     def ring_forward(first, buf, off, pos, dev):
         first[0].wait_recv()
-        part = buf.at[off((pos + 3) % SIDE), low]
+        part = view(buf, off((pos + 3) % SIDE), low)
         up = rcopy(part, part, dev(1))
         first[1].wait_recv()
-        part = buf.at[off((pos + 1) % SIDE), high]
+        part = view(buf, off((pos + 1) % SIDE), high)
         down = rcopy(part, part, dev(3))
         return [up, down]
 
@@ -158,26 +162,27 @@
         for c in copies:
             c.wait_send()
 
-    w2_off = lambda j: rows_of(hp * j, hp)
+    w2_off = lambda j: j
     w13_off = lambda j: rows_of(h2 * j, h2)
     row_off = lambda b: rows_of(rb * b, rb)
     ext_off = lambda b: rows_of(rb * b + main, 16)
     w13_src = w_hbm.at[pl.ds(0, h2)]
     my_pre = pl.ds(pl.multiple_of(q * rp, 128), rp)
 
-    w2_copies = ring_start(w2_hbm, w2, w2_off, q, dev_q)
-    strip = pre_hbm.shape[1] // 2
+    w2_copies = ring_start(w3_hbm.at[2], w2, w2_off, q, dev_q)
+    w13_copies = ring_start(w13_src, w13, w13_off, q, dev_q)
+    strip = pre_hbm.shape[2] // 2
     local = [
         pltpu.make_async_copy(
-            pre_hbm.at[:, pl.ds(i * strip, strip)],
-            stage.at[pl.ds(i * h2, h2), pl.ds(0, strip)],
+            pre_hbm.at[i % 2, :, pl.ds(i // 2 * strip, strip)],
+            stage.at[i, :, pl.ds(0, strip)],
             local_sem.at[i],
         )
-        for i in (0, 1)
+        for i in range(4)
     ]
     local += [
-        pltpu.make_async_copy(w2_hbm, w2.at[w2_off(q)], local_sem.at[2]),
-        pltpu.make_async_copy(w13_src, w13.at[w13_off(q)], local_sem.at[3]),
+        pltpu.make_async_copy(w3_hbm.at[2], w2.at[w2_off(q)], local_sem.at[4]),
+        pltpu.make_async_copy(w13_src, w13.at[w13_off(q)], local_sem.at[5]),
     ]
     for c in local:
         c.start()
@@ -253,7 +258,6 @@
                 unfold_ref[pl.ds(16 * j, 16), :], small_got[...], ((1,), (0,))
             ).astype(BF16)
 
-    xmain = stage.at[pl.ds(2 * h2, main), pl.ds(0, width)]
     dispatch(gout_ref, probs, gmain, gext)
     g_sent = exchange(gmain, gext, g_buf, gext_got)
     dispatch(tok_ref, None, xmain, xext)
@@ -261,24 +265,29 @@
     g_buf[blank, :] = jnp.zeros((rp - rows, width), BF16)
     x_buf[blank, :] = jnp.zeros((rp - rows, width), BF16)
 
-    local[0].wait()
-    local[1].wait()
+    for c in local[:4]:
+        c.wait()
     span = rp // 3
     line = lax.broadcasted_iota(jnp.int32, (span, span), 0)
     lane = lax.broadcasted_iota(jnp.int32, (span, span), 1)
 
     def regroup(to, _):
         for n in range(3):
-            total = jnp.zeros((h2, span), F32)
+            total = [jnp.zeros((h, span), F32)] * 2
             source = lmap_ref[0:1, pl.ds(n * span, span)]
             for b in (n, n + 1):
                 block = core * (SIDE * b + to) + (1 - core) * (SIDE * to + b)
                 start = rb * (block % 8)
-                window = stage[rows_of(block // 8 * h2, h2), cols_of(start // 128 * 128, span)]
+                window = cols_of(start // 128 * 128, span)
                 at = lane + (n * span - rb * b)
                 match = (at >= 0) & (at < rb) & (line - start % 128 == source)
-                total += dot(window, match.astype(F32).astype(BF16), ((1,), (0,)))
-            dgt[rows_of(h2 * to, h2), pl.ds(n * span, span)] = total.astype(BF16)
+                match = match.astype(F32).astype(BF16)
+                total = [
+                    total[i] + dot(stage[block // 8 * 2 + i, :, window], match, ((1,), (0,)))
+                    for i in (0, 1)
+                ]
+            both = jnp.concatenate(total, 0).astype(BF16)
+            dgt[rows_of(h2 * to, h2), pl.ds(n * span, span)] = both
         return 0
 
     lax.fori_loop(0, SIDE, regroup, 0)
@@ -289,7 +298,6 @@
     own_pre = pltpu.make_async_copy(dgt.at[rows_of(h2 * q, h2)], pre.at[:, my_pre], local_sem.at[0])
     own_pre.start()
 
-    w13_copies = ring_start(w13_src, w13, w13_off, q, dev_q)
     w2_copies += ring_forward(w2_copies, w2, w2_off, q, dev_q)
 
     wait_recv(g_sent)
@@ -305,8 +313,8 @@
 
     wait_send(g_sent)
     signal(credit_z, [dev_e(d) for d in range(1, experts)])
-    local[2].wait()
-    local[3].wait()
+    local[4].wait()
+    local[5].wait()
     wait_recv(w2_copies[2:])
     wait_recv(g_copies[2:])
 
@@ -314,11 +322,12 @@
 
     def back_step(n, _):
         cols = cols_of(n * nc, nc)
-        acc[...] += dot(w2[:, cols], g_buf[:, cols], ((1,), (1,)))
+        rows_g = g_buf[:, cols]
+        for j in range(SIDE):
+            acc[pl.ds(h * j, h), :] += dot(w2[j, :, cols], rows_g, ((1,), (1,)))
         return 0
 
     lax.fori_loop(0, steps, back_step, 0)
-    x_copies += ring_forward(x_copies, x_buf, row_off, p, dev_p)
     wait_recv(pre_copies)
     wait_send(pre_copies)
     own_pre.wait()
@@ -327,7 +336,7 @@
         j, c = i // (rp // 128), i % (rp // 128)
         lanes = cols_of(c * 128, 128)
         saved = pre[:, cols_of(j * rp + c * 128, 128)].astype(F32)
-        back = acc[rows_of(hp * j, hp), lanes][:h]
+        back = acc[pl.ds(pl.multiple_of(h * j, 8), h), lanes]
         a, b = saved[:h], saved[h:]
         sig = jax.nn.sigmoid(a)
         act = a * sig
@@ -346,25 +355,30 @@
     def send_far(part, off, pos, dst, dev):
         far = off((pos + 2) % SIDE)
         return [
-            rcopy(part.at[far, low], dst.at[:, low], dev(1)),
-            rcopy(part.at[far, high], dst.at[:, high], dev(3)),
+            rcopy(view(part, far, low), dst.at[:, low], dev(1)),
+            rcopy(view(part, far, high), dst.at[:, high], dev(3)),
         ]
 
     def send_near_direct(part, off, pos, dst, dev):
         return [
-            rcopy(part.at[off((pos + 1) % SIDE), high], dst[0].at[:, high], dev(1)),
-            rcopy(part.at[off((pos + 3) % SIDE), low], dst[1].at[:, low], dev(3)),
+            rcopy(view(part, off((pos + 1) % SIDE), high), dst[0].at[:, high], dev(1)),
+            rcopy(view(part, off((pos + 3) % SIDE), low), dst[1].at[:, low], dev(3)),
         ]
 
-    def add_into(part, where, others, start, size):
+    def add_into(part, where, others, start, size, out=None):
         ac = 256 if half % 256 == 0 else 128
 
         def add_step(n, _):
             cols = cols_of(start + n * ac, ac)
-            total = part[where, cols].astype(F32)
+            mine = view(part, where, cols)
+            total = mine[...].astype(F32)
             for ref in others:
                 total = total + ref[:, cols].astype(F32)
-            part[where, cols] = total.astype(BF16)
+            if out is None:
+                mine[...] = total.astype(BF16)
+            else:
+                for i in (0, 1):
+                    out[i][:, cols] = total[h * i : h * (i + 1)].astype(BF16)
             return 0
 
         lax.fori_loop(0, size // ac, add_step, 0)
@@ -373,26 +387,28 @@
         far[0].wait_recv()
         where = off((pos + 1) % SIDE)
         add_into(part, where, [got], 0, half)
-        up = rcopy(part.at[where, low], dst[0].at[:, low], dev(1))
+        up = rcopy(view(part, where, low), dst[0].at[:, low], dev(1))
         far[1].wait_recv()
         where = off((pos + 3) % SIDE)
         add_into(part, where, [got], half, half)
-        down = rcopy(part.at[where, high], dst[1].at[:, high], dev(3))
+        down = rcopy(view(part, where, high), dst[1].at[:, high], dev(3))
         return [up, down]
 
     wait_send(x_sent)
 
     def dw2_step(n, _):
         cols = cols_of(n * nc, nc)
-        stage[pl.ds(0, SIDE * hp), cols] = dot(sct[...], g_buf[:, cols], ((1,), (0,))).astype(BF16)
+        part = dot(sct[...], g_buf[:, cols], ((1,), (0,)))
+        for j in range(SIDE):
+            stage[j, :, cols] = part[hp * j : hp * j + h].astype(BF16)
         return 0
 
     lax.fori_loop(0, steps, dw2_step, 0)
     pl.semaphore_wait(credit_a, 2)
-    dw2_near = [w2.at[pl.ds(hp, hp)], w2.at[pl.ds(2 * hp, hp)]]
-    dw2_far_got = w2.at[pl.ds(0, hp)]
+    dw2_near = [w2.at[1], w2.at[2]]
+    dw2_far_got = w2.at[0]
     dw2_far = send_far(stage, w2_off, q, dw2_far_got, dev_q)
-    dw2_mid = send_near_direct(stage, w2_off, q, dw2_near, dev_q)
+    x_copies += ring_forward(x_copies, x_buf, row_off, p, dev_p)
 
     def flip(c, _):
         lanes = cols_of(c * 128, 128)
@@ -400,7 +416,6 @@
         return 0
 
     lax.fori_loop(0, rp // 128, flip, 0)
-    dw2_mid += send_near_added(dw2_far, stage, w2_off, q, dw2_far_got, dw2_near, dev_q)
 
     wait_send(g_copies)
     wait_recv(w13_copies[2:])
@@ -424,6 +439,8 @@
     dx_mid = send_near_direct(g_buf, row_off, p, dx_near, dev_p)
     dx_block(0)
     dx_mid += send_near_added(dx_far, g_buf, row_off, p, dx_far_got, dx_near, dev_p)
+    dw2_mid = send_near_direct(stage, w2_off, q, dw2_near, dev_q)
+    dw2_mid += send_near_added(dw2_far, stage, w2_off, q, dw2_far_got, dw2_near, dev_q)
 
     wait_recv(x_copies[2:])
     wait_send(w13_copies)
@@ -451,8 +468,6 @@
     signal(credit_b, [dev_q(1), dev_q(3)])
     pl.semaphore_wait(credit_b, 2)
     dw13_mid = send_near_direct(w13, w13_off, q, dw13_near, dev_q)
-    dw13_mid += send_near_added(dw13_far, w13, w13_off, q, dw13_far_got, dw13_near, dev_q)
-
     wait_recv(dx_mid)
     add_into(g_buf, row_off(p), dx_near, 0, width)
     folded = jnp.zeros((experts * 16, piece), F32)
@@ -478,12 +493,13 @@
     gmain[rows_of(mb * e, mb), :] = g_buf[my_slots, :]
     rext_got[rows_of(16 * e, 16), :] = rext[rows_of(16 * e, 16), :]
 
+    dw13_mid += send_near_added(dw13_far, w13, w13_off, q, dw13_far_got, dw13_near, dev_q)
+
     wait_recv(dw2_mid)
     add_into(stage, w2_off(q), dw2_near, 0, width)
-    out2 = pltpu.make_async_copy(
-        stage.at[w2_off(q), pl.ds(0, width)], dw_hbm.at[pl.ds(h2, hp)], local_sem.at[0]
-    )
-    out2.start()
+    full = pl.ds(0, width)
+    outs = [pltpu.make_async_copy(stage.at[q, :, full], dw_hbm.at[2], local_sem.at[2])]
+    outs[0].start()
 
     wait_recv(ret)
     for j in range(pieces):
@@ -492,14 +508,17 @@
         total += dot(home_ext[pl.ds(j * tokens, tokens), :], rext_got[...], ((1,), (0,)))
         gt_ref[:, cols] = total.astype(BF16)
 
+    wait_send(dw2_far + dw2_mid)
     wait_recv(dw13_mid)
-    add_into(w13, w13_off(q), dw13_near, 0, width)
-    out13 = pltpu.make_async_copy(w13.at[w13_off(q)], dw_hbm.at[pl.ds(0, h2)], local_sem.at[1])
-    out13.start()
-
-    wait_send(dw2_far + dw2_mid + dx_far + dx_mid + dw13_far + dw13_mid + ret)
-    out2.wait()
-    out13.wait()
+    sums = [stage.at[(q + 1 + i) % SIDE] for i in (0, 1)]
+    add_into(w13, w13_off(q), dw13_near, 0, width, sums)
+    for i in (0, 1):
+        outs.append(pltpu.make_async_copy(sums[i].at[:, full], dw_hbm.at[i], local_sem.at[i]))
+        outs[-1].start()
+
+    wait_send(dx_far + dx_mid + dw13_far + dw13_mid + ret)
+    for c in outs:
+        c.wait()
 
 
 def on_device(tokens, grad_out, route_probs, expert_ids, saved_pre, expert_weights):
@@ -515,9 +534,8 @@
     rp = round_up(SIDE * rb + 64, 128)
     strip = saved_pre.shape[1] // 2
     pieces = max(k for k in range(1, 16 // xb + 1) if width % (128 * k) == 0)
-    w = jnp.transpose(expert_weights[0], (1, 2, 0)).reshape(3 * hidden, width)
-    w2 = lax.pad(w, jnp.zeros((), BF16), ((-2 * hidden, hp - hidden, 0), (0, 0, 0)))
-    pre = jnp.transpose(saved_pre[0], (1, 2, 0)).reshape(2 * hidden, saved_pre.shape[1])
+    w3 = jnp.transpose(expert_weights[0], (1, 2, 0))
+    pre = jnp.transpose(saved_pre[0], (1, 2, 0))
 
     at = np.arange(rb)
     in_main = at // mb * cap + at % mb
@@ -537,7 +555,7 @@
         functools.partial(kernel, cap, pieces),
         out_shape=(
             jax.ShapeDtypeStruct((rows, width), BF16),
-            jax.ShapeDtypeStruct((2 * hidden + hp, width), BF16),
+            jax.ShapeDtypeStruct((3, hidden, width), BF16),
         ),
         in_specs=[vmem] * 7 + [hbm] * 3,
         out_specs=(vmem, hbm),
@@ -545,13 +563,14 @@
             pltpu.VMEM((rp, width), BF16),
             pltpu.VMEM((rp, width), BF16),
             pltpu.VMEM((SIDE * 2 * hidden, width), BF16),
-            pltpu.VMEM((SIDE * hp, width), BF16),
+            pltpu.VMEM((SIDE, hidden, width), BF16),
             pltpu.VMEM((2 * hidden, SIDE * rp), BF16),
             pltpu.VMEM((SIDE * 2 * hidden, rp), BF16),
             pltpu.VMEM((rp, SIDE * 2 * hidden), BF16),
             pltpu.VMEM((SIDE * hp, rp), BF16),
-            pltpu.VMEM((SIDE * hp, rp), F32),
-            pltpu.VMEM((4 * hidden + main, max(width, strip)), BF16),
+            pltpu.VMEM((SIDE * hidden, rp), F32),
+            pltpu.VMEM((SIDE, hidden, max(width, strip)), BF16),
+            pltpu.VMEM((main, width), BF16),
             pltpu.VMEM((main, width), BF16),
             pltpu.VMEM((3 * rb, width), BF16),
             pltpu.VMEM((experts * 16, width // pieces), BF16),
@@ -564,7 +583,7 @@
             pltpu.VMEM((pieces * rows, experts * 16), BF16),
             pltpu.SemaphoreType.DMA((N_COPIES,)),
             pltpu.SemaphoreType.DMA((N_COPIES,)),
-            pltpu.SemaphoreType.DMA((5,)),
+            pltpu.SemaphoreType.DMA((6,)),
             pltpu.SemaphoreType.REGULAR,
             pltpu.SemaphoreType.REGULAR,
             pltpu.SemaphoreType.REGULAR,
@@ -581,12 +600,11 @@
         jnp.asarray(lmap),
         jnp.asarray(fold, BF16),
         jnp.asarray(unfold, BF16),
-        w,
-        w2,
+        w3.reshape(3 * hidden, width),
+        w3,
         pre,
     )
-    grad = dw[: 3 * hidden].reshape(3, hidden, width)
-    return gt, jnp.transpose(grad, (2, 0, 1))[None]
+    return gt, jnp.transpose(dw, (2, 0, 1))[None]
 
 
 def solution(mesh):

time: 247 us -> 239 us (0.968)
  Pallas kernels: 239 us -> 233 us
    pallas_call x1, Pallas kernels: 239 us -> 233 us  [on_device(): pl.pallas_call(functools.partial(kernel, cap, pieces), out_shape=(jax.Sha...]
    unnamed x3 -> x2, local copies, waits for them, and re-layouts: 0.93 us -> 6 us
    slice x1 -> x0, local copies, waits for them, and re-layouts: 3.92 us -> none  [on_device(): grad = dw[:3 * hidden].reshape(3, hidden, width)]
where the time goes in v3:
time: 239 us
  Pallas kernels  233 us (97%)
  local copies, waits for them, and re-layouts  6 us (3%)
    pallas_call x1, Pallas kernels, on_device(): pl.pallas_call(functools.partial(kernel, cap, pieces), out_shape=(jax.Sha...  233 us
    unnamed x2, local copies, waits for them, and re-layouts  6 us

profile of v3, /device:TPU:1, one launch (start us, length us, event | category | flops | bytes accessed | tf_op | source)
XLA Modules:
  0.0 239.1 jit_solution(2470980717117021522)
XLA Ops:
  0.6 232.5 %experts_backward.1 = (bf16[128,3584]{1,0:T(8,128)(2,1)}, bf16[3,152,3584]{2,1,0:T(8,128)(2,1)}) custom-call(s32[2,128]{1,0:T(2,128)} %bitcast.17, bf16[2,128]{1,0:T(2,128)(2,1)} %bitcast.18, bf16[128,3584]{1,0:T(8,128)(2,1)} %gout_ref.1, bf16[128,3584]{1,0:T(8,128)(2,1)} %tok_ref.1, s32[8,1152]{1,0:T(8,128)} %constant.6.clone.lmap_ref, ...), custom_call_target="tpu_custom_call" | custom-call | tf_op jit(solution)/shard_map/experts_backward/pallas_call | solution.py:554
  233.1 2.2 copy.13
  235.3 3.8 %copy.14 = bf16[1,3584,3,152]{1,3,2,0:T(8,128)(2,1)} copy(bf16[1,3584,3,152]{1,3,2,0:T(8,128)(2,1)} %bitcast.15) | data formatting | bytes 6537216

commit v4 on v3

--- a/solution.py
+++ b/solution.py
@@ -142,8 +142,10 @@
         return ref.at[where, :, cols] if len(ref.shape) == 3 else ref.at[where, cols]
 
     def ring_start(src, buf, off, pos, dev):
-        mine = buf.at[off(pos)]
-        return [rcopy(src, mine, dev(1)), rcopy(src, mine, dev(3))]
+        return [
+            rcopy(src.at[:, cols], view(buf, off(pos), cols), dev(d))
+            for d, cols in ((1, low), (3, high), (1, high), (3, low))
+        ]
 
     def ring_forward(first, buf, off, pos, dev):
         first[0].wait_recv()

time: 239 us -> 237 us (level)
  Pallas kernels: 233 us -> 230 us
where the time goes in v4:
time: 237 us
  Pallas kernels  230 us (97%)
  local copies, waits for them, and re-layouts  6 us (3%)
    pallas_call x1, Pallas kernels, on_device(): pl.pallas_call(functools.partial(kernel, cap, pieces), out_shape=(jax.Sha...  230 us
    unnamed x2, local copies, waits for them, and re-layouts  6 us

profile of v4, /device:TPU:1, one launch (start us, length us, event | category | flops | bytes accessed | tf_op | source)
XLA Modules:
  0.0 237.0 jit_solution(9656151262598680014)
XLA Ops:
  0.6 230.4 %experts_backward.1 = (bf16[128,3584]{1,0:T(8,128)(2,1)}, bf16[3,152,3584]{2,1,0:T(8,128)(2,1)}) custom-call(s32[2,128]{1,0:T(2,128)} %bitcast.17, bf16[2,128]{1,0:T(2,128)(2,1)} %bitcast.18, bf16[128,3584]{1,0:T(8,128)(2,1)} %gout_ref.1, bf16[128,3584]{1,0:T(8,128)(2,1)} %tok_ref.1, s32[8,1152]{1,0:T(8,128)} %constant.6.clone.lmap_ref, ...), custom_call_target="tpu_custom_call" | custom-call | tf_op jit(solution)/shard_map/experts_backward/pallas_call | solution.py:556
  231.0 2.2 copy.13
  233.2 3.8 %copy.14 = bf16[1,3584,3,152]{1,3,2,0:T(8,128)(2,1)} copy(bf16[1,3584,3,152]{1,3,2,0:T(8,128)(2,1)} %bitcast.15) | data formatting | bytes 6537216

commit v5 on v4

--- a/solution.py
+++ b/solution.py
@@ -470,8 +470,10 @@
     signal(credit_b, [dev_q(1), dev_q(3)])
     pl.semaphore_wait(credit_b, 2)
     dw13_mid = send_near_direct(w13, w13_off, q, dw13_near, dev_q)
-    wait_recv(dx_mid)
-    add_into(g_buf, row_off(p), dx_near, 0, width)
+    wait_recv(dx_mid[1:3])
+    add_into(g_buf, row_off(p), dx_near, 0, half)
+    wait_recv([dx_mid[0], dx_mid[3]])
+    add_into(g_buf, row_off(p), dx_near, half, half)
     folded = jnp.zeros((experts * 16, piece), F32)
     for j in range(pieces):
         folded += dot(
@@ -511,12 +513,17 @@
         gt_ref[:, cols] = total.astype(BF16)
 
     wait_send(dw2_far + dw2_mid)
-    wait_recv(dw13_mid)
     sums = [stage.at[(q + 1 + i) % SIDE] for i in (0, 1)]
-    add_into(w13, w13_off(q), dw13_near, 0, width, sums)
-    for i in (0, 1):
-        outs.append(pltpu.make_async_copy(sums[i].at[:, full], dw_hbm.at[i], local_sem.at[i]))
-        outs[-1].start()
+    for part, cols in ((0, low), (1, high)):
+        wait_recv(dw13_mid[1:3] if part == 0 else [dw13_mid[0], dw13_mid[3]])
+        add_into(w13, w13_off(q), dw13_near, part * half, half, sums)
+        for i in (0, 1):
+            outs.append(
+                pltpu.make_async_copy(
+                    sums[i].at[:, cols], dw_hbm.at[i, :, cols], local_sem.at[3 * part + i]
+                )
+            )
+            outs[-1].start()
 
     wait_send(dx_far + dx_mid + dw13_far + dw13_mid + ret)
     for c in outs:

time: 237 us -> 237 us (level)
  no operation moved by 1% of the time
where the time goes in v5:
time: 237 us
  Pallas kernels  230 us (97%)
  local copies, waits for them, and re-layouts  6 us (3%)
    pallas_call x1, Pallas kernels, on_device(): pl.pallas_call(functools.partial(kernel, cap, pieces), out_shape=(jax.Sha...  230 us
    unnamed x2, local copies, waits for them, and re-layouts  6 us

profile of v5, /device:TPU:1, one launch (start us, length us, event | category | flops | bytes accessed | tf_op | source)
XLA Modules:
  0.0 236.7 jit_solution(9985676427860478852)
XLA Ops:
  0.6 230.1 %experts_backward.1 = (bf16[128,3584]{1,0:T(8,128)(2,1)}, bf16[3,152,3584]{2,1,0:T(8,128)(2,1)}) custom-call(s32[2,128]{1,0:T(2,128)} %bitcast.17, bf16[2,128]{1,0:T(2,128)(2,1)} %bitcast.18, bf16[128,3584]{1,0:T(8,128)(2,1)} %gout_ref.1, bf16[128,3584]{1,0:T(8,128)(2,1)} %tok_ref.1, s32[8,1152]{1,0:T(8,128)} %constant.6.clone.lmap_ref, ...), custom_call_target="tpu_custom_call" | custom-call | tf_op jit(solution)/shard_map/experts_backward/pallas_call | solution.py:563
  230.7 2.2 copy.13
  232.9 3.8 %copy.14 = bf16[1,3584,3,152]{1,3,2,0:T(8,128)(2,1)} copy(bf16[1,3584,3,152]{1,3,2,0:T(8,128)(2,1)} %bitcast.15) | data formatting | bytes 6537216
